TPU v7x, 32 devices: a whole 2x2x4 slice. The times are simulated.
32 devices in a mesh: row: 32 (over z, y, x, core), col: 1.
Axes of the slice: x: 2, y: 2, z: 4, core: 2. Of those that a mesh axis runs over, the one named last changes fastest.
Arguments:
- left_factors: bfloat16 [1536, 32, 512], P('col', None, 'row'), may hold values from -0.15625 to 0.15625
- right_factors: bfloat16 [1536, 4, 512], P('col'), may hold values from -0.15625 to 0.15625
- amplitudes: bfloat16 [64, 512, 512], P('col', 'row'), may hold values from -0.46875 to 0.46875
Outputs:
- ladder: float32 [64, 32, 4], P('col', 'row')
All inputs are finite; a program needn't handle non-finite values.
Results may differ from a plain program's by a relative error of at most 0.0029.
Values may be sent and summed in bfloat16 or wider, within the bound.
A program may use at most 64 MiB of HBM per device.

v0:
```python
import jax
import jax.numpy as jnp
from jax import lax
from jax.sharding import PartitionSpec as P


def contract_aux(left_part, right_part):
    return lax.dot_general(
        left_part, right_part, (((0,), (0,)), ((), ())), preferred_element_type=jnp.float32
    )


def per_device(left_factors, right_factors, amplitudes):
    count_a = left_factors.shape[1]
    c_block = left_factors.shape[2]
    count_b = right_factors.shape[1]
    width = right_factors.shape[2]
    pairs = amplitudes.shape[0]
    left_full = lax.all_gather(left_factors, "col", axis=0, tiled=True)
    left_flat = left_full.reshape(left_full.shape[0], count_a * c_block)
    right_full = lax.all_gather(right_factors, "col", axis=0, tiled=True)
    tile = contract_aux(left_flat, right_full.reshape(right_full.shape[0], count_b * width))
    rounded = tile.astype(jnp.bfloat16).reshape(count_a, c_block, count_b, width)
    matrix = jnp.transpose(rounded, (1, 3, 0, 2)).reshape(c_block * width, count_a * count_b)
    flat_amps = amplitudes.reshape(pairs, c_block * width)
    partial_value = jnp.dot(flat_amps, matrix, preferred_element_type=jnp.float32)
    partial_value = partial_value.reshape(pairs, count_a, count_b)
    return lax.psum_scatter(partial_value, "row", scatter_dimension=1, tiled=True)


def solution(mesh):
    placed = (P("col", None, "row"), P("col", None, None), P("col", "row", None))
    return jax.shard_map(
        per_device, mesh=mesh, in_specs=placed, out_specs=P("col", "row", None), check_vma=False
    )
```

profile of v0, /device:TPU:0, one launch (start us, length us, event | category | flops | bytes accessed | tf_op | source)
XLA Modules:
  0.0 62.9 jit_solution(16339274956188022173)
XLA Ops:
  0.0 0.0 copy-start
  0.0 5.6 %copy.9 = bf16[192,8,4,512]{3,1,2,0:T(8,128)(2,1)S(1)} copy(bf16[192,8,4,512]{3,2,1,0:T(4,128)(2,1)} %bitcast.21) | data formatting | bytes 12582912
  5.6 0.0 copy-done
  5.6 4.6 %convolution_convert_fusion = bf16[512,2048]{1,0:T(8,128)(2,1)} fusion(bf16[1536,512]{0,1:T(8,128)(2,1)S(1)} %bitcast.18, bf16[1536,2048]{1,0:T(8,128)(2,1)S(1)} %bitcast.22), kind=kOutput, calls=%fused_computation | convolution fusion | flops 3222274048 | bytes 9961472 | tf_op jit(solution)/shard_map/dot_general | solution.py:8
  10.2 4.5 %reshape.20 = bf16[32,16,4,512]{3,2,1,0:T(4,128)(2,1)} reshape(bf16[512,2048]{1,0:T(8,128)(2,1)} %convolution_convert_fusion) | data formatting | bytes 4194304 | tf_op jit(solution)/shard_map/reshape | solution.py:23
  14.7 2.2 %copy.7 = bf16[32,16,4,512]{3,1,2,0:T(8,128)(2,1)S(1)} copy(bf16[32,16,4,512]{3,2,1,0:T(4,128)(2,1)} %reshape.20) | data formatting | bytes 4194304 | tf_op jit(solution)/shard_map/reshape | solution.py:23
  17.0 0.0 copy-start.1
  17.0 1.4 %copy.10 = bf16[16,8,16,512]{3,1,2,0:T(8,128)(2,1)S(1)} copy(bf16[16,8,16,512]{3,2,1,0:T(8,128)(2,1)S(1)} %bitcast.20) | data formatting | bytes 4194304
  18.4 0.0 copy-done.1
  18.4 0.6 copy.11
  19.0 0.8 %convolution_bitcast_fusion = f32[64,128]{1,0:T(8,128)S(1)} fusion(bf16[8192,128]{0,1:T(8,128)(2,1)S(1)} %bitcast.19, bf16[64,8192]{1,0:T(8,128)(2,1)S(1)} %bitcast.23), kind=kOutput, calls=%fused_computation.1 | convolution fusion | flops 134217728 | bytes 3178496 | tf_op jit(solution)/shard_map/dot_general | solution.py:26
  19.9 0.1 copy.8
  20.0 42.3 %all-reduce = f32[64,32,4]{0,2,1:T(4,128)S(1)} all-reduce(f32[64,32,4]{0,2,1:T(4,128)S(1)} %bitcast.25), channel_id=2, replica_groups=mesh['row'=32,'col'=1] {'row'}, use_global_device_ids=true, to_apply=%region_0.0.clone | all-reduce | flops 8192 | bytes 65536
  62.3 0.6 constant_dynamic-slice_fusion
Async XLA Ops:
  0.0 5.6 %copy-start = (bf16[1536,32,16]{0,2,1:T(8,128)(2,1)S(1)}, bf16[1536,32,16]{0,2,1:T(8,128)(2,1)}, u32[]{:S(2)}) copy-start(bf16[1536,32,16]{0,2,1:T(8,128)(2,1)} %param.3) | copy-start | bytes 4718596
  17.0 1.4 %copy-start.1 = (bf16[64,16,512]{2,1,0:T(8,128)(2,1)S(1)}, bf16[64,16,512]{2,1,0:T(8,128)(2,1)}, u32[]{:S(2)}) copy-start(bf16[64,16,512]{2,1,0:T(8,128)(2,1)} %param.5) | copy-start | bytes 3145732
where the time goes:
time: 63.2 us; the launch traced here: 62.9 us
  blocking collectives  42.3 us (67%)
  local copies, waits for them, and re-layouts  15 us (24%)
  matrix products  5.48 us (9%)
    unnamed x1, blocking collectives  42.3 us
    unnamed x8, local copies, waits for them, and re-layouts  8.19 us
    reshape x2, local copies, waits for them, and re-layouts, per_device(): tile.astype(jnp.bfloat16).reshape(count_a, c_block, count_b, width)  6.73 us
    dot_general x1, matrix products, contract_aux(): lax.dot_general(left_part, right_part, (((0,), (0,)), ((), ())), preferre...  4.63 us

commit v1 on v0

v1 whole, which is shorter than its diff:
```python
import functools

import jax
import jax.numpy as jnp
from jax import lax
from jax.experimental import pallas as pl
from jax.experimental.pallas import tpu as pltpu
from jax.sharding import PartitionSpec as P

MESH = pl.DeviceIdType.MESH
LANES = 128


def ladder_kernel(
    n, fold, left_hbm, right_hbm, amps_hbm, out_ref,
    left_in, amps_in, right_in, left_f32, amps_f32, left_rows, amps_rows, right_cols,
    integrals, send_buf, recv_buf, load_sem, send_sem, recv_sem,
):
    count_a, c_block, naux = left_hbm.shape
    _, count_b, width = right_hbm.shape
    pairs = amps_hbm.shape[0]
    chunks = width // LANES
    own_a = count_a // n
    me = lax.axis_index("row")

    load_left = pltpu.make_async_copy(left_hbm, left_in, load_sem.at[0])
    load_amps = pltpu.make_async_copy(amps_hbm, amps_in, load_sem.at[1])
    load_right = [
        pltpu.make_async_copy(
            right_hbm.at[:, :, pl.ds(k * LANES, LANES)], right_in.at[k], load_sem.at[2 + k]
        )
        for k in range(chunks)
    ]
    load_left.start()
    for k in range(chunks // 2):
        load_right[k].start()
    load_amps.start()
    for k in range(chunks // 2, chunks):
        load_right[k].start()

    barrier = pltpu.get_barrier_semaphore()

    @pl.loop(1, n)
    def _(k):
        pl.semaphore_signal(
            barrier, inc=1, device_id={"row": lax.rem(me + k, n)}, device_id_type=MESH
        )

    load_left.wait()
    for k in range(naux // LANES):
        lanes = pl.ds(k * LANES, LANES)
        left_f32[k % 2] = left_in[:, :, lanes].astype(jnp.float32).reshape(count_a * c_block, LANES)
        for c in range(c_block):
            left_rows[pl.ds(c * count_a, count_a), lanes] = left_f32[
                k % 2, pl.ds(c, count_a, stride=c_block), :
            ].astype(jnp.bfloat16)

    rows = 256
    q_rows = rows // count_b
    i = lax.broadcasted_iota(jnp.int32, (rows, rows), 0)
    j = lax.broadcasted_iota(jnp.int32, (rows, rows), 1)
    pick = (j == (i % q_rows) * count_b + i // q_rows).astype(jnp.bfloat16)

    half = 2 * LANES
    total = None
    for h in range(width // half):
        load_right[2 * h].wait()
        load_right[2 * h + 1].wait()
        for s in range(naux // q_rows):
            part = jnp.concatenate(
                [
                    right_in[2 * h + e, pl.ds(s * q_rows, q_rows)].reshape(rows, LANES)
                    for e in range(2)
                ],
                axis=1,
            )
            moved = jnp.dot(pick, part, preferred_element_type=jnp.float32).astype(jnp.bfloat16)
            for b in range(count_b):
                right_cols[h % 2, pl.ds(s * q_rows, q_rows), pl.ds(b * half, half)] = moved[
                    b * q_rows : (b + 1) * q_rows
                ]
        for b in range(count_b):
            cols = pl.ds(b * half, half)
            integrals[h % 2, :, cols] = jnp.dot(
                left_rows[...], right_cols[h % 2, :, cols], preferred_element_type=jnp.float32
            ).astype(jnp.bfloat16)
        if h == 0:
            load_amps.wait()
            for k in range(chunks):
                lanes = pl.ds(k * LANES, LANES)
                amps_f32[k % 2] = amps_in[:, :, lanes].astype(jnp.float32).reshape(
                    pairs * c_block, LANES
                )
                for c in range(c_block):
                    picked = amps_f32[k % 2, pl.ds(c, pairs, stride=c_block), :].astype(jnp.bfloat16)
                    for f in range(fold):
                        amps_rows[c, pl.ds(f * pairs, pairs), lanes] = picked
        for c in range(c_block):
            block = jnp.concatenate(
                [
                    integrals[h % 2, pl.ds(c * count_a, count_a), pl.ds(b * half, half)]
                    for b in range(count_b)
                ],
                axis=0,
            )
            term = lax.dot_general(
                block, amps_rows[c, :, pl.ds(h * half, half)], (((1,), (1,)), ((), ())),
                preferred_element_type=jnp.float32,
            )
            total = term if total is None else total + term

    lane = lax.broadcasted_iota(jnp.int32, (count_a, fold * pairs), 1)
    for g in range(count_b // fold):
        row = total[g * fold * count_a : (g * fold + 1) * count_a]
        for f in range(1, fold):
            b = g * fold + f
            row = jnp.where(lane >= f * pairs, total[b * count_a : (b + 1) * count_a], row)
        send_buf[:, g, :] = row

    pl.semaphore_wait(barrier, n - 1)

    @pl.loop(1, n)
    def _(k):
        to = lax.rem(me + k, n)
        pltpu.make_async_remote_copy(
            src_ref=send_buf.at[pl.ds(to * own_a, own_a)],
            dst_ref=recv_buf.at[pl.ds((k - 1) * own_a, own_a)],
            send_sem=send_sem,
            recv_sem=recv_sem,
            device_id={"row": to},
            device_id_type=MESH,
        ).start()

    every = recv_buf.at[pl.ds(0, (n - 1) * own_a)]
    pltpu.make_async_copy(every, every, recv_sem).wait()
    mine = send_buf[pl.ds(me * own_a, own_a)]
    got = recv_buf[...].reshape((n - 1, own_a) + recv_buf.shape[1:])
    result = mine + jnp.sum(got, axis=0)
    for b in range(count_b):
        out_ref[:, b, :] = result[:, b // fold, (b % fold) * pairs : (b % fold + 1) * pairs]
    pltpu.make_async_copy(every, every, send_sem).wait()


def per_device(n, left_factors, right_factors, amplitudes):
    left = lax.all_gather(left_factors, "col", axis=0, tiled=True)
    right = lax.all_gather(right_factors, "col", axis=0, tiled=True)
    naux, count_a, c_block = left.shape
    _, count_b, width = right.shape
    pairs = amplitudes.shape[0]
    fold = 2 if 2 * pairs == LANES and count_b % 2 == 0 else 1
    own_a = count_a // n
    half = 2 * LANES
    anywhere = pl.BlockSpec(memory_space=pl.ANY)
    bf16, f32 = jnp.bfloat16, jnp.float32
    piece = (count_b // fold, fold * pairs)
    out = pl.pallas_call(
        functools.partial(ladder_kernel, n, fold),
        out_shape=jax.ShapeDtypeStruct((own_a, count_b, pairs), f32),
        in_specs=[anywhere] * 3,
        out_specs=pl.BlockSpec(memory_space=pltpu.VMEM),
        scratch_shapes=[
            pltpu.VMEM((count_a, c_block, naux), bf16),
            pltpu.VMEM((pairs, c_block, width), bf16),
            pltpu.VMEM((width // LANES, naux, count_b, LANES), bf16),
            pltpu.VMEM((2, count_a * c_block, LANES), f32),
            pltpu.VMEM((2, pairs * c_block, LANES), f32),
            pltpu.VMEM((c_block * count_a, naux), bf16),
            pltpu.VMEM((c_block, fold * pairs, width), bf16),
            pltpu.VMEM((2, naux, count_b * half), bf16),
            pltpu.VMEM((2, c_block * count_a, count_b * half), bf16),
            pltpu.VMEM((count_a,) + piece, f32),
            pltpu.VMEM(((n - 1) * own_a,) + piece, f32),
            pltpu.SemaphoreType.DMA((2 + width // LANES,)),
            pltpu.SemaphoreType.DMA,
            pltpu.SemaphoreType.DMA,
        ],
        compiler_params=pltpu.CompilerParams(
            collective_id=0, has_side_effects=True, vmem_limit_bytes=48 * 1024 * 1024
        ),
        name="ladder",
    )(jnp.transpose(left, (1, 2, 0)), right, amplitudes)
    return jnp.transpose(out, (2, 0, 1))


def solution(mesh):
    placed = (P("col", None, "row"), P("col", None, None), P("col", "row", None))
    return jax.shard_map(
        functools.partial(per_device, mesh.shape["row"]),
        mesh=mesh, in_specs=placed, out_specs=P("col", "row", None), check_vma=False,
    )
```

time: 63.2 us -> 21.6 us (0.34)
  blocking collectives: 42.3 us -> 0 us
  Pallas kernels: 0 us -> 18.2 us
  local copies, waits for them, and re-layouts: 15 us -> 3.21 us
  matrix products: 5.48 us -> 0 us
    unnamed x1 -> x0, blocking collectives: 42.3 us -> none
    pallas_call x0 -> x1, Pallas kernels: none -> 18.2 us  [per_device(): pl.pallas_call(functools.partial(ladder_kernel, n, fold), out_shape=jax.S...]
    reshape x2 -> x0, local copies, waits for them, and re-layouts: 6.73 us -> none  [per_device(): tile.astype(jnp.bfloat16).reshape(count_a, c_block, count_b, width)]
    dot_general x2 -> x0, matrix products: 5.48 us -> none  [the longest x1 4.63 us: contract_aux(): lax.dot_general(left_part, right_part, (((0,), (0,)), ((), ())), preferre...]
    unnamed x8 -> x5, local copies, waits for them, and re-layouts: 8.19 us -> 3.21 us
where the time goes in v1:
time: 21.6 us; the launch traced here: 21.4 us
  Pallas kernels  18.2 us (84%)
  local copies, waits for them, and re-layouts  3.21 us (15%)
    pallas_call x1, Pallas kernels, per_device(): pl.pallas_call(functools.partial(ladder_kernel, n, fold), out_shape=jax.S...  18.2 us
    unnamed x5, local copies, waits for them, and re-layouts  3.21 us

profile of v1, /device:TPU:0, one launch (start us, length us, event | category | flops | bytes accessed | tf_op | source)
XLA Modules:
  0.0 21.4 jit_solution(1769337850172189368)
XLA Ops:
  0.0 0.0 copy-start
  0.0 1.4 %copy-done = bf16[1536,32,16]{0,2,1:T(8,128)(2,1)S(1)} copy-done((bf16[1536,32,16]{0,2,1:T(8,128)(2,1)S(1)}, bf16[1536,32,16]{0,2,1:T(8,128)(2,1)}, u32[]{:S(2)}) %copy-start) | copy-done | bytes 1572888
  1.4 0.0 copy-start.1
  1.4 1.2 %copy-done.1 = bf16[64,16,512]{2,1,0:T(8,128)(2,1)S(1)} copy-done((bf16[64,16,512]{2,1,0:T(8,128)(2,1)S(1)}, bf16[64,16,512]{2,1,0:T(8,128)(2,1)}, u32[]{:S(2)}) %copy-start.1) | copy-done | bytes 1048600
  2.6 18.2 %ladder.1 = f32[1,4,64]{2,1,0:T(4,128)S(1)} custom-call(bf16[32,16,1536]{2,1,0:T(8,128)(2,1)S(1)} %bitcast.2, bf16[1536,4,512]{2,1,0:T(4,128)(2,1)} %right_hbm, bf16[64,16,512]{2,1,0:T(8,128)(2,1)S(1)} %copy-done.1), custom_call_target="tpu_custom_call" | custom-call | tf_op jit(solution)/shard_map/ladder/pallas_call | solution.py:156
  20.8 0.6 %copy.5 = f32[64,1,4]{0,2,1:T(4,128)} copy(f32[64,1,4]{0,2,1:T(4,128)S(1)} %bitcast.3) | data formatting | bytes 2048
Async XLA Ops:
  0.0 1.4 %copy-start = (bf16[1536,32,16]{0,2,1:T(8,128)(2,1)S(1)}, bf16[1536,32,16]{0,2,1:T(8,128)(2,1)}, u32[]{:S(2)}) copy-start(bf16[1536,32,16]{0,2,1:T(8,128)(2,1)} %param.3) | copy-start | bytes 4718596
  1.4 1.2 %copy-start.1 = (bf16[64,16,512]{2,1,0:T(8,128)(2,1)S(1)}, bf16[64,16,512]{2,1,0:T(8,128)(2,1)}, u32[]{:S(2)}) copy-start(bf16[64,16,512]{2,1,0:T(8,128)(2,1)} %amps_hbm.1) | copy-start | bytes 3145732

commit v2 on v1

--- a/solution.py
+++ b/solution.py
@@ -13,7 +13,7 @@
 
 def ladder_kernel(
     n, fold, left_hbm, right_hbm, amps_hbm, out_ref,
-    left_in, amps_in, right_in, left_f32, amps_f32, left_rows, amps_rows, right_cols,
+    left_in, amps_in, right_in, left_f32, left_rows, amps_f32, amps_rows, right_f32, right_cols,
     integrals, send_buf, recv_buf, load_sem, send_sem, recv_sem,
 ):
     count_a, c_block, naux = left_hbm.shape
@@ -21,6 +21,7 @@
     pairs = amps_hbm.shape[0]
     chunks = width // LANES
     own_a = count_a // n
+    deep = 2 if c_block % 2 == 0 else 1
     me = lax.axis_index("row")
 
     load_left = pltpu.make_async_copy(left_hbm, left_in, load_sem.at[0])
@@ -55,59 +56,75 @@
                 k % 2, pl.ds(c, count_a, stride=c_block), :
             ].astype(jnp.bfloat16)
 
-    rows = 256
-    q_rows = rows // count_b
-    i = lax.broadcasted_iota(jnp.int32, (rows, rows), 0)
-    j = lax.broadcasted_iota(jnp.int32, (rows, rows), 1)
-    pick = (j == (i % q_rows) * count_b + i // q_rows).astype(jnp.bfloat16)
-
-    half = 2 * LANES
-    total = None
-    for h in range(width // half):
-        load_right[2 * h].wait()
-        load_right[2 * h + 1].wait()
-        for s in range(naux // q_rows):
-            part = jnp.concatenate(
-                [
-                    right_in[2 * h + e, pl.ds(s * q_rows, q_rows)].reshape(rows, LANES)
-                    for e in range(2)
-                ],
-                axis=1,
-            )
-            moved = jnp.dot(pick, part, preferred_element_type=jnp.float32).astype(jnp.bfloat16)
+    def split_right(k):
+        staged, columns = right_f32[k % 2], right_cols[k % 2]
+        flat = right_in.at[k].reshape(naux * count_b, LANES)
+        step = 64
+        for s in range(naux // step):
+            rows = pl.ds(s * step * count_b, step * count_b)
+            staged[rows, :] = flat[rows, :].astype(jnp.float32)
             for b in range(count_b):
-                right_cols[h % 2, pl.ds(s * q_rows, q_rows), pl.ds(b * half, half)] = moved[
-                    b * q_rows : (b + 1) * q_rows
-                ]
-        for b in range(count_b):
-            cols = pl.ds(b * half, half)
-            integrals[h % 2, :, cols] = jnp.dot(
-                left_rows[...], right_cols[h % 2, :, cols], preferred_element_type=jnp.float32
+                columns[pl.ds(s * step, step), pl.ds(b * LANES, LANES)] = staged[
+                    pl.ds(s * step * count_b + b, step, stride=count_b), :
+                ].astype(jnp.bfloat16)
+
+    def split_amps(k):
+        lanes = pl.ds(k * LANES, LANES)
+        staged = amps_f32[k % 2]
+        staged[...] = amps_in[:, :, lanes].astype(jnp.float32).reshape(pairs * c_block, LANES)
+        for c in range(c_block):
+            picked = staged[pl.ds(c, pairs, stride=c_block), :].astype(jnp.bfloat16)
+            for f in range(fold):
+                amps_rows[k % 2][
+                    c // deep, pl.ds(f * pairs, pairs), pl.ds((c % deep) * LANES, LANES)
+                ] = picked
+
+    def integrate(k):
+        for b in range(0, count_b, 2):
+            cols = pl.ds(b * LANES, min(2, count_b - b) * LANES)
+            integrals[k % 2][:, cols] = jnp.dot(
+                left_rows[...], right_cols[k % 2][:, cols], preferred_element_type=jnp.float32
             ).astype(jnp.bfloat16)
-        if h == 0:
-            load_amps.wait()
-            for k in range(chunks):
-                lanes = pl.ds(k * LANES, LANES)
-                amps_f32[k % 2] = amps_in[:, :, lanes].astype(jnp.float32).reshape(
-                    pairs * c_block, LANES
-                )
-                for c in range(c_block):
-                    picked = amps_f32[k % 2, pl.ds(c, pairs, stride=c_block), :].astype(jnp.bfloat16)
-                    for f in range(fold):
-                        amps_rows[c, pl.ds(f * pairs, pairs), lanes] = picked
-        for c in range(c_block):
+
+    def contract(k, total):
+        for g in range(c_block // deep):
             block = jnp.concatenate(
                 [
-                    integrals[h % 2, pl.ds(c * count_a, count_a), pl.ds(b * half, half)]
+                    jnp.concatenate(
+                        [
+                            integrals[k % 2][
+                                pl.ds((g * deep + e) * count_a, count_a), pl.ds(b * LANES, LANES)
+                            ]
+                            for e in range(deep)
+                        ],
+                        axis=1,
+                    )
                     for b in range(count_b)
                 ],
                 axis=0,
             )
             term = lax.dot_general(
-                block, amps_rows[c, :, pl.ds(h * half, half)], (((1,), (1,)), ((), ())),
+                block, amps_rows[k % 2][g], (((1,), (1,)), ((), ())),
                 preferred_element_type=jnp.float32,
             )
             total = term if total is None else total + term
+        return total
+
+    load_right[0].wait()
+    split_right(0)
+    total = None
+    for k in range(chunks):
+        if k + 1 < chunks:
+            load_right[k + 1].wait()
+        if k == 0:
+            load_amps.wait()
+        integrate(k)
+        if k + 1 < chunks:
+            split_right(k + 1)
+        if k > 0:
+            total = contract(k - 1, total)
+        split_amps(k)
+    total = contract(chunks - 1, total)
 
     lane = lax.broadcasted_iota(jnp.int32, (count_a, fold * pairs), 1)
     for g in range(count_b // fold):
@@ -149,7 +166,7 @@
     pairs = amplitudes.shape[0]
     fold = 2 if 2 * pairs == LANES and count_b % 2 == 0 else 1
     own_a = count_a // n
-    half = 2 * LANES
+    deep = 2 if c_block % 2 == 0 else 1
     anywhere = pl.BlockSpec(memory_space=pl.ANY)
     bf16, f32 = jnp.bfloat16, jnp.float32
     piece = (count_b // fold, fold * pairs)
@@ -163,11 +180,12 @@
             pltpu.VMEM((pairs, c_block, width), bf16),
             pltpu.VMEM((width // LANES, naux, count_b, LANES), bf16),
             pltpu.VMEM((2, count_a * c_block, LANES), f32),
-            pltpu.VMEM((2, pairs * c_block, LANES), f32),
             pltpu.VMEM((c_block * count_a, naux), bf16),
-            pltpu.VMEM((c_block, fold * pairs, width), bf16),
-            pltpu.VMEM((2, naux, count_b * half), bf16),
-            pltpu.VMEM((2, c_block * count_a, count_b * half), bf16),
+            [pltpu.VMEM((pairs * c_block, LANES), f32)] * 2,
+            [pltpu.VMEM((c_block // deep, fold * pairs, deep * LANES), bf16)] * 2,
+            [pltpu.VMEM((naux * count_b, LANES), f32)] * 2,
+            [pltpu.VMEM((naux, count_b * LANES), bf16)] * 2,
+            [pltpu.VMEM((c_block * count_a, count_b * LANES), bf16)] * 2,
             pltpu.VMEM((count_a,) + piece, f32),
             pltpu.VMEM(((n - 1) * own_a,) + piece, f32),
             pltpu.SemaphoreType.DMA((2 + width // LANES,)),
@@ -175,7 +193,7 @@
             pltpu.SemaphoreType.DMA,
         ],
         compiler_params=pltpu.CompilerParams(
-            collective_id=0, has_side_effects=True, vmem_limit_bytes=48 * 1024 * 1024
+            collective_id=0, has_side_effects=True, vmem_limit_bytes=62 * 1024 * 1024
         ),
         name="ladder",
     )(jnp.transpose(left, (1, 2, 0)), right, amplitudes)

time: 21.6 us -> 21.4 us (level)
  local copies, waits for them, and re-layouts: 3.21 us -> 1.26 us
  Pallas kernels: 18.2 us -> 20 us
    unnamed x5 -> x1, local copies, waits for them, and re-layouts: 3.21 us -> 1.26 us
    pallas_call x1, Pallas kernels: 18.2 us -> 20 us  [per_device(): pl.pallas_call(functools.partial(ladder_kernel, n, fold), out_shape=jax.S...]
where the time goes in v2:
time: 21.4 us; the launch traced here: 21.2 us
  Pallas kernels  20 us (93%)
  local copies, waits for them, and re-layouts  1.26 us (6%)
    pallas_call x1, Pallas kernels, per_device(): pl.pallas_call(functools.partial(ladder_kernel, n, fold), out_shape=jax.S...  20 us
    unnamed x1, local copies, waits for them, and re-layouts  1.26 us

profile of v2, /device:TPU:0, one launch (start us, length us, event | category | flops | bytes accessed | tf_op | source)
XLA Modules:
  0.0 21.2 jit_solution(2565640467210752726)
XLA Ops:
  0.0 20.0 %ladder.1 = f32[1,4,64]{2,1,0:T(4,128)} custom-call(bf16[32,16,1536]{2,1,0:T(8,128)(2,1)} %bitcast.2, bf16[1536,4,512]{2,1,0:T(4,128)(2,1)} %right_hbm, bf16[64,16,512]{2,1,0:T(8,128)(2,1)} %amps_hbm.1), custom_call_target="tpu_custom_call" | custom-call | tf_op jit(solution)/shard_map/ladder/pallas_call | solution.py:173
  20.0 1.3 %copy.5 = f32[64,1,4]{0,2,1:T(4,128)} copy(f32[64,1,4]{0,2,1:T(4,128)} %bitcast.3) | data formatting | bytes 2048

commit v3 on v2

--- a/solution.py
+++ b/solution.py
@@ -26,18 +26,19 @@
 
     load_left = pltpu.make_async_copy(left_hbm, left_in, load_sem.at[0])
     load_amps = pltpu.make_async_copy(amps_hbm, amps_in, load_sem.at[1])
-    load_right = [
-        pltpu.make_async_copy(
-            right_hbm.at[:, :, pl.ds(k * LANES, LANES)], right_in.at[k], load_sem.at[2 + k]
+
+    def load_right(k):
+        lanes = pl.ds(pl.multiple_of(k * LANES, LANES), LANES)
+        return pltpu.make_async_copy(
+            right_hbm.at[:, :, lanes], right_in.at[k], load_sem.at[2 + k]
         )
-        for k in range(chunks)
-    ]
+
     load_left.start()
     for k in range(chunks // 2):
-        load_right[k].start()
+        load_right(k).start()
     load_amps.start()
     for k in range(chunks // 2, chunks):
-        load_right[k].start()
+        load_right(k).start()
 
     barrier = pltpu.get_barrier_semaphore()
 
@@ -48,16 +49,22 @@
         )
 
     load_left.wait()
-    for k in range(naux // LANES):
-        lanes = pl.ds(k * LANES, LANES)
-        left_f32[k % 2] = left_in[:, :, lanes].astype(jnp.float32).reshape(count_a * c_block, LANES)
-        for c in range(c_block):
-            left_rows[pl.ds(c * count_a, count_a), lanes] = left_f32[
-                k % 2, pl.ds(c, count_a, stride=c_block), :
-            ].astype(jnp.bfloat16)
-
-    def split_right(k):
-        staged, columns = right_f32[k % 2], right_cols[k % 2]
+    left_lanes = naux // LANES
+    turn = 2 if left_lanes % 2 == 0 else 1
+
+    @pl.loop(0, left_lanes // turn)
+    def _(t):
+        for e in range(turn):
+            lanes = pl.ds(pl.multiple_of((t * turn + e) * LANES, LANES), LANES)
+            staged = left_f32[e]
+            staged[...] = left_in[:, :, lanes].astype(jnp.float32).reshape(count_a * c_block, LANES)
+            for c in range(c_block):
+                left_rows[pl.ds(c * count_a, count_a), lanes] = staged[
+                    pl.ds(c, count_a, stride=c_block), :
+                ].astype(jnp.bfloat16)
+
+    def split_right(k, slot):
+        staged, columns = right_f32[slot], right_cols[slot]
         flat = right_in.at[k].reshape(naux * count_b, LANES)
         step = 64
         for s in range(naux // step):
@@ -68,31 +75,32 @@
                     pl.ds(s * step * count_b + b, step, stride=count_b), :
                 ].astype(jnp.bfloat16)
 
-    def split_amps(k):
-        lanes = pl.ds(k * LANES, LANES)
-        staged = amps_f32[k % 2]
+    def split_amps(k, slot):
+        lanes = pl.ds(pl.multiple_of(k * LANES, LANES), LANES)
+        staged = amps_f32[slot]
         staged[...] = amps_in[:, :, lanes].astype(jnp.float32).reshape(pairs * c_block, LANES)
         for c in range(c_block):
             picked = staged[pl.ds(c, pairs, stride=c_block), :].astype(jnp.bfloat16)
             for f in range(fold):
-                amps_rows[k % 2][
+                amps_rows[slot][
                     c // deep, pl.ds(f * pairs, pairs), pl.ds((c % deep) * LANES, LANES)
                 ] = picked
 
-    def integrate(k):
+    def integrate(slot):
         for b in range(0, count_b, 2):
             cols = pl.ds(b * LANES, min(2, count_b - b) * LANES)
-            integrals[k % 2][:, cols] = jnp.dot(
-                left_rows[...], right_cols[k % 2][:, cols], preferred_element_type=jnp.float32
+            integrals[slot][:, cols] = jnp.dot(
+                left_rows[...], right_cols[slot][:, cols], preferred_element_type=jnp.float32
             ).astype(jnp.bfloat16)
 
-    def contract(k, total):
+    def contract(slot):
+        total = None
         for g in range(c_block // deep):
             block = jnp.concatenate(
                 [
                     jnp.concatenate(
                         [
-                            integrals[k % 2][
+                            integrals[slot][
                                 pl.ds((g * deep + e) * count_a, count_a), pl.ds(b * LANES, LANES)
                             ]
                             for e in range(deep)
@@ -104,27 +112,34 @@
                 axis=0,
             )
             term = lax.dot_general(
-                block, amps_rows[k % 2][g], (((1,), (1,)), ((), ())),
+                block, amps_rows[slot][g], (((1,), (1,)), ((), ())),
                 preferred_element_type=jnp.float32,
             )
             total = term if total is None else total + term
         return total
 
-    load_right[0].wait()
-    split_right(0)
-    total = None
-    for k in range(chunks):
-        if k + 1 < chunks:
-            load_right[k + 1].wait()
-        if k == 0:
-            load_amps.wait()
-        integrate(k)
-        if k + 1 < chunks:
-            split_right(k + 1)
-        if k > 0:
-            total = contract(k - 1, total)
-        split_amps(k)
-    total = contract(chunks - 1, total)
+    load_right(0).wait()
+    split_right(0, 0)
+    integrals[1][...] = jnp.zeros_like(integrals[1])
+    amps_rows[1][...] = jnp.zeros_like(amps_rows[1])
+    load_amps.wait()
+
+    def step(k, slot, total):
+        @pl.when(k + 1 < chunks)
+        def _():
+            load_right(k + 1).wait()
+
+        integrate(slot)
+        split_right(lax.rem(k + 1, chunks), 1 - slot)
+        total = total + contract(1 - slot)
+        split_amps(k, slot)
+        return total
+
+    total = lax.fori_loop(
+        0, chunks // 2, lambda t, total: step(2 * t + 1, 1, step(2 * t, 0, total)),
+        jnp.zeros((count_b * count_a, fold * pairs), jnp.float32),
+    )
+    total = total + contract(1)
 
     lane = lax.broadcasted_iota(jnp.int32, (count_a, fold * pairs), 1)
     for g in range(count_b // fold):
@@ -179,7 +194,7 @@
             pltpu.VMEM((count_a, c_block, naux), bf16),
             pltpu.VMEM((pairs, c_block, width), bf16),
             pltpu.VMEM((width // LANES, naux, count_b, LANES), bf16),
-            pltpu.VMEM((2, count_a * c_block, LANES), f32),
+            [pltpu.VMEM((count_a * c_block, LANES), f32)] * 2,
             pltpu.VMEM((c_block * count_a, naux), bf16),
             [pltpu.VMEM((pairs * c_block, LANES), f32)] * 2,
             [pltpu.VMEM((c_block // deep, fold * pairs, deep * LANES), bf16)] * 2,
@@ -193,7 +208,7 @@
             pltpu.SemaphoreType.DMA,
         ],
         compiler_params=pltpu.CompilerParams(
-            collective_id=0, has_side_effects=True, vmem_limit_bytes=62 * 1024 * 1024
+            collective_id=0, has_side_effects=True, vmem_limit_bytes=53 * 1024 * 1024
         ),
         name="ladder",
     )(jnp.transpose(left, (1, 2, 0)), right, amplitudes)

time: 21.4 us -> 21.5 us (level)
  Pallas kernels: 20 us -> 20.8 us
  local copies, waits for them, and re-layouts: 1.26 us -> 0.58 us
    pallas_call x1, Pallas kernels: 20 us -> 20.8 us  [per_device(): pl.pallas_call(functools.partial(ladder_kernel, n, fold), out_shape=jax.S...]
    unnamed x1, local copies, waits for them, and re-layouts: 1.26 us -> 0.58 us
where the time goes in v3:
time: 21.5 us; the launch traced here: 21.4 us
  Pallas kernels  20.8 us (97%)
  local copies, waits for them, and re-layouts  0.58 us (3%)
    pallas_call x1, Pallas kernels, per_device(): pl.pallas_call(functools.partial(ladder_kernel, n, fold), out_shape=jax.S...  20.8 us
    unnamed x1, local copies, waits for them, and re-layouts  0.58 us

profile of v3, /device:TPU:0, one launch (start us, length us, event | category | flops | bytes accessed | tf_op | source)
XLA Modules:
  0.0 21.4 jit_solution(5557456875219566261)
XLA Ops:
  0.0 20.8 %ladder.1 = f32[1,4,64]{2,1,0:T(4,128)S(1)} custom-call(bf16[32,16,1536]{2,1,0:T(8,128)(2,1)} %bitcast.3, bf16[1536,4,512]{2,1,0:T(4,128)(2,1)} %right_hbm, bf16[64,16,512]{2,1,0:T(8,128)(2,1)} %amps_hbm.1), custom_call_target="tpu_custom_call" | custom-call | tf_op jit(solution)/shard_map/ladder/pallas_call | solution.py:188
  20.8 0.6 %copy.5 = f32[64,1,4]{0,2,1:T(4,128)} copy(f32[64,1,4]{0,2,1:T(4,128)S(1)} %bitcast.2) | data formatting | bytes 2048

commit v4 on v2

v4 whole, which is shorter than its diff:
```python
import functools

import jax
import jax.numpy as jnp
from jax import lax
from jax.experimental import pallas as pl
from jax.experimental.pallas import tpu as pltpu
from jax.sharding import PartitionSpec as P

MESH = pl.DeviceIdType.MESH
LANES = 128
TILE = 256
LEFT_PIECES = 3


def ladder_kernel(
    n, fold, left_hbm, right_hbm, amps_hbm, out_ref,
    left_in, amps_in, right_in, left_f32, left_rows, amps_f32, amps_rows, right_f32, right_cols,
    integrals, total_buf, send_buf, recv_buf, load_sem, send_sem, recv_sem,
):
    count_a, c_block, naux = left_hbm.shape
    _, count_b, width = right_hbm.shape
    pairs = amps_hbm.shape[0]
    chunks = width // LANES
    own_a = count_a // n
    me = lax.axis_index("row")

    left_lanes = naux // LANES
    q_tiles = naux // TILE
    m_halves = count_a * c_block // TILE

    def load_left(p):
        lanes = pl.ds(p * (naux // LEFT_PIECES), naux // LEFT_PIECES)
        return pltpu.make_async_copy(
            left_hbm.at[:, :, lanes], left_in.at[:, :, lanes], load_sem.at[1 + chunks + p]
        )

    load_amps = pltpu.make_async_copy(amps_hbm, amps_in, load_sem.at[0])

    def load_right(k):
        lanes = pl.ds(pl.multiple_of(k * LANES, LANES), LANES)
        return pltpu.make_async_copy(
            right_hbm.at[:, :, lanes], right_in.at[k], load_sem.at[1 + k]
        )

    for p in range(LEFT_PIECES):
        load_left(p).start()
    for k in range(chunks // 2):
        load_right(k).start()
    load_amps.start()
    for k in range(chunks // 2, chunks):
        load_right(k).start()

    barrier = pltpu.get_barrier_semaphore()

    @pl.loop(1, n)
    def _(k):
        pl.semaphore_signal(
            barrier, inc=1, device_id={"row": lax.rem(me + k, n)}, device_id_type=MESH
        )

    turn = 2
    for p in range(LEFT_PIECES):
        load_left(p).wait()

        @pl.loop(0, left_lanes // (LEFT_PIECES * turn))
        def _(t):
            for e in range(turn):
                at = p * (left_lanes // LEFT_PIECES) + t * turn + e
                lanes = pl.ds(pl.multiple_of(at * LANES, LANES), LANES)
                staged = left_f32[e]
                staged[...] = (
                    left_in[:, :, lanes].astype(jnp.float32).reshape(count_a * c_block, LANES)
                )
                for c in range(c_block):
                    left_rows[pl.ds(c * count_a, count_a), lanes] = staged[
                        pl.ds(c, count_a, stride=c_block), :
                    ].astype(jnp.bfloat16)

    def split_right(k, kt):
        staged, columns = right_f32[k % 2], right_cols[k % 2]
        flat = right_in.at[k].reshape(naux * count_b, LANES)
        step = 64
        for s in range(kt * TILE // step, (kt + 1) * TILE // step):
            rows = pl.ds(s * step * count_b, step * count_b)
            staged[rows, :] = flat[rows, :].astype(jnp.float32)
            for b in range(count_b):
                columns[pl.ds(s * step, step), pl.ds(b * LANES, LANES)] = staged[
                    pl.ds(s * step * count_b + b, step, stride=count_b), :
                ].astype(jnp.bfloat16)

    def split_amps(k, kt):
        lanes = pl.ds(k * LANES, LANES)
        staged = amps_f32[k % 2]
        if kt == 0:
            staged[...] = amps_in[:, :, lanes].astype(jnp.float32).reshape(pairs * c_block, LANES)
        for c in range(kt * c_block // q_tiles, (kt + 1) * c_block // q_tiles):
            picked = staged[pl.ds(c, pairs, stride=c_block), :].astype(jnp.bfloat16)
            for f in range(fold):
                amps_rows[k % 2][
                    pl.ds(((c // 2) * fold + f) * pairs, pairs), pl.ds((c % 2) * LANES, LANES)
                ] = picked

    def block_of(k, g):
        return jnp.concatenate(
            [
                jnp.concatenate(
                    [
                        integrals[k % 2][
                            pl.ds((g * 2 + e) * count_a, count_a), pl.ds(b * LANES, LANES)
                        ]
                        for e in range(2)
                    ],
                    axis=1,
                )
                for b in range(count_b)
            ],
            axis=0,
        )

    def integrate(acc, k, kt):
        def push(m, staging):
            pltpu.matmul_push_rhs(
                right_cols[k % 2][pl.ds(kt * TILE, TILE), pl.ds(m * TILE, TILE)], staging, m
            )

        def multiply(m, staging):
            for h in range(m_halves):
                pltpu.matmul_acc_lhs(
                    acc[m][h], left_rows[pl.ds(h * TILE, TILE), pl.ds(kt * TILE, TILE)],
                    load_staged_rhs=staging if h == 0 else None,
                )

        def finish():
            if kt == q_tiles - 1:
                for h in range(m_halves):
                    for m in range(2):
                        integrals[k % 2][pl.ds(h * TILE, TILE), pl.ds(m * TILE, TILE)] = (
                            pltpu.matmul_pop(acc[m][h]).astype(jnp.bfloat16)
                        )

        return push, multiply, finish

    def contract(acc_out, k, p):
        def push(m, staging):
            pltpu.matmul_push_rhs(
                amps_rows[k % 2][pl.ds((2 * p + m) * TILE, TILE), :], staging, m, transpose=True
            )

        def multiply(m, staging):
            for e in range(2):
                pltpu.matmul_acc_lhs(
                    acc_out[m][e], block_of(k, 2 * (2 * p + m) + e),
                    load_staged_rhs=staging if e == 0 else None,
                )

        return push, multiply, lambda: None

    def arrived(k):
        if k + 1 < chunks:
            load_right(k + 1).wait()
        if k == 0:
            load_amps.wait()

    def on_units(acc, acc_out):
        tiles = []
        for k in range(chunks):
            for kt in range(q_tiles):
                beside = []
                if k + 1 < chunks:
                    beside.append(functools.partial(split_right, k + 1, kt))
                beside.append(functools.partial(split_amps, k, kt))
                before = functools.partial(arrived, k) if kt == 0 else None
                tiles.append((integrate(acc, k, kt), before, beside))
                if k > 0 and kt in (1, 2):
                    tiles.append((contract(acc_out, k - 1, kt - 1), None, []))
        tiles += [(contract(acc_out, chunks - 1, p), None, []) for p in range(2)]

        load_right(0).wait()
        for kt in range(q_tiles):
            split_right(0, kt)
        for m in range(2):
            tiles[0][0][0](m, 0)
        for i, ((_, multiply, finish), before, beside) in enumerate(tiles):
            if before is not None:
                before()
            if i + 1 < len(tiles):
                for m in range(2):
                    tiles[i + 1][0][0](m, (i + 1) % 2)
            for m in range(2):
                multiply(m, i % 2)
            for run in beside:
                run()
            finish()
        total = 0.0
        for m in range(2):
            for e in range(2):
                total += pltpu.matmul_pop(acc_out[m][e])[:, e * LANES : (e + 1) * LANES]
        total_buf[...] = total

    pl.run_scoped(
        on_units,
        [[pltpu.ACC(m)((TILE, TILE), jnp.float32)] * m_halves for m in range(2)],
        [[pltpu.ACC(m)((count_a * count_b, TILE), jnp.float32)] * 2 for m in range(2)],
    )
    total = total_buf[...]

    lane = lax.broadcasted_iota(jnp.int32, (count_a, fold * pairs), 1)
    for g in range(count_b // fold):
        row = total[g * fold * count_a : (g * fold + 1) * count_a]
        for f in range(1, fold):
            b = g * fold + f
            row = jnp.where(lane >= f * pairs, total[b * count_a : (b + 1) * count_a], row)
        send_buf[:, g, :] = row

    pl.semaphore_wait(barrier, n - 1)

    @pl.loop(1, n)
    def _(k):
        to = lax.rem(me + k, n)
        pltpu.make_async_remote_copy(
            src_ref=send_buf.at[pl.ds(to * own_a, own_a)],
            dst_ref=recv_buf.at[pl.ds((k - 1) * own_a, own_a)],
            send_sem=send_sem,
            recv_sem=recv_sem,
            device_id={"row": to},
            device_id_type=MESH,
        ).start()

    every = recv_buf.at[pl.ds(0, (n - 1) * own_a)]
    pltpu.make_async_copy(every, every, recv_sem).wait()
    mine = send_buf[pl.ds(me * own_a, own_a)]
    got = recv_buf[...].reshape((n - 1, own_a) + recv_buf.shape[1:])
    result = mine + jnp.sum(got, axis=0)
    for b in range(count_b):
        out_ref[:, b, :] = result[:, b // fold, (b % fold) * pairs : (b % fold + 1) * pairs]
    pltpu.make_async_copy(every, every, send_sem).wait()


def per_device(n, left_factors, right_factors, amplitudes):
    left = lax.all_gather(left_factors, "col", axis=0, tiled=True)
    right = lax.all_gather(right_factors, "col", axis=0, tiled=True)
    naux, count_a, c_block = left.shape
    _, count_b, width = right.shape
    pairs = amplitudes.shape[0]
    fold = 2 if 2 * pairs == LANES and count_b % 2 == 0 else 1
    own_a = count_a // n
    anywhere = pl.BlockSpec(memory_space=pl.ANY)
    bf16, f32 = jnp.bfloat16, jnp.float32
    piece = (count_b // fold, fold * pairs)
    out = pl.pallas_call(
        functools.partial(ladder_kernel, n, fold),
        out_shape=jax.ShapeDtypeStruct((own_a, count_b, pairs), f32),
        in_specs=[anywhere] * 3,
        out_specs=pl.BlockSpec(memory_space=pltpu.VMEM),
        scratch_shapes=[
            pltpu.VMEM((count_a, c_block, naux), bf16),
            pltpu.VMEM((pairs, c_block, width), bf16),
            pltpu.VMEM((width // LANES, naux, count_b, LANES), bf16),
            [pltpu.VMEM((count_a * c_block, LANES), f32)] * 2,
            pltpu.VMEM((c_block * count_a, naux), bf16),
            [pltpu.VMEM((pairs * c_block, LANES), f32)] * 2,
            [pltpu.VMEM((c_block // 2 * fold * pairs, TILE), bf16)] * 2,
            [pltpu.VMEM((naux * count_b, LANES), f32)] * 2,
            [pltpu.VMEM((naux, count_b * LANES), bf16)] * 2,
            [pltpu.VMEM((c_block * count_a, count_b * LANES), bf16)] * 2,
            pltpu.VMEM((count_b * count_a, fold * pairs), f32),
            pltpu.VMEM((count_a,) + piece, f32),
            pltpu.VMEM(((n - 1) * own_a,) + piece, f32),
            pltpu.SemaphoreType.DMA((1 + width // LANES + LEFT_PIECES,)),
            pltpu.SemaphoreType.DMA,
            pltpu.SemaphoreType.DMA,
        ],
        compiler_params=pltpu.CompilerParams(
            collective_id=0, has_side_effects=True, vmem_limit_bytes=53 * 1024 * 1024
        ),
        name="ladder",
    )(jnp.transpose(left, (1, 2, 0)), right, amplitudes)
    return jnp.transpose(out, (2, 0, 1))


def solution(mesh):
    placed = (P("col", None, "row"), P("col", None, None), P("col", "row", None))
    return jax.shard_map(
        functools.partial(per_device, mesh.shape["row"]),
        mesh=mesh, in_specs=placed, out_specs=P("col", "row", None), check_vma=False,
    )
```

time: 21.4 us -> 18.7 us (0.87)
  Pallas kernels: 20 us -> 18 us
  local copies, waits for them, and re-layouts: 1.26 us -> 0.58 us
    pallas_call x1, Pallas kernels: 20 us -> 18 us  [per_device(): pl.pallas_call(functools.partial(ladder_kernel, n, fold), out_shape=jax.S...]
    unnamed x1, local copies, waits for them, and re-layouts: 1.26 us -> 0.58 us
where the time goes in v4:
time: 18.7 us; the launch traced here: 18.6 us
  Pallas kernels  18 us (96%)
  local copies, waits for them, and re-layouts  0.58 us (3%)
    pallas_call x1, Pallas kernels, per_device(): pl.pallas_call(functools.partial(ladder_kernel, n, fold), out_shape=jax.S...  18 us
    unnamed x1, local copies, waits for them, and re-layouts  0.58 us

profile of v4, /device:TPU:0, one launch (start us, length us, event | category | flops | bytes accessed | tf_op | source)
XLA Modules:
  0.0 18.6 jit_solution(13852448318211294030)
XLA Ops:
  0.0 18.0 %ladder.1 = f32[1,4,64]{2,1,0:T(4,128)S(1)} custom-call(bf16[32,16,1536]{2,1,0:T(8,128)(2,1)} %bitcast.3, bf16[1536,4,512]{2,1,0:T(4,128)(2,1)} %right_hbm, bf16[64,16,512]{2,1,0:T(8,128)(2,1)} %amps_hbm.1), custom_call_target="tpu_custom_call" | custom-call | tf_op jit(solution)/shard_map/ladder/pallas_call | solution.py:251
  18.0 0.6 %copy.5 = f32[64,1,4]{0,2,1:T(4,128)} copy(f32[64,1,4]{0,2,1:T(4,128)S(1)} %bitcast.2) | data formatting | bytes 2048

commit v5 on v4

--- a/solution.py
+++ b/solution.py
@@ -10,13 +10,12 @@
 MESH = pl.DeviceIdType.MESH
 LANES = 128
 TILE = 256
-LEFT_PIECES = 3
 
 
 def ladder_kernel(
     n, fold, left_hbm, right_hbm, amps_hbm, out_ref,
-    left_in, amps_in, right_in, left_f32, left_rows, amps_f32, amps_rows, right_f32, right_cols,
-    integrals, total_buf, send_buf, recv_buf, load_sem, send_sem, recv_sem,
+    left_in, amps_in, right_in, left_f32, left_rows, amps_f32, amps_rows, right_f32,
+    integrals, total_buf, send_buf, recv_buf, left_sem, right_sem, amps_sem, send_sem, recv_sem,
 ):
     count_a, c_block, naux = left_hbm.shape
     _, count_b, width = right_hbm.shape
@@ -25,31 +24,30 @@
     own_a = count_a // n
     me = lax.axis_index("row")
 
-    left_lanes = naux // LANES
     q_tiles = naux // TILE
     m_halves = count_a * c_block // TILE
 
-    def load_left(p):
-        lanes = pl.ds(p * (naux // LEFT_PIECES), naux // LEFT_PIECES)
+    def load_left(kt):
+        lanes = pl.ds(kt * TILE, TILE)
         return pltpu.make_async_copy(
-            left_hbm.at[:, :, lanes], left_in.at[:, :, lanes], load_sem.at[1 + chunks + p]
-        )
-
-    load_amps = pltpu.make_async_copy(amps_hbm, amps_in, load_sem.at[0])
-
-    def load_right(k):
-        lanes = pl.ds(pl.multiple_of(k * LANES, LANES), LANES)
+            left_hbm.at[:, :, lanes], left_in.at[:, :, lanes], left_sem.at[kt]
+        )
+
+    def load_right(k, kt):
+        rows = pl.ds(kt * TILE, TILE) if k == 0 else slice(None)
         return pltpu.make_async_copy(
-            right_hbm.at[:, :, lanes], right_in.at[k], load_sem.at[1 + k]
-        )
-
-    for p in range(LEFT_PIECES):
-        load_left(p).start()
-    for k in range(chunks // 2):
-        load_right(k).start()
-    load_amps.start()
-    for k in range(chunks // 2, chunks):
-        load_right(k).start()
+            right_hbm.at[rows, :, pl.ds(k * LANES, LANES)], right_in.at[k, rows],
+            right_sem.at[kt if k == 0 else q_tiles - 1 + k],
+        )
+
+    load_amps = pltpu.make_async_copy(amps_hbm, amps_in, amps_sem)
+    for kt in range(q_tiles):
+        load_left(kt).start()
+        load_right(0, kt).start()
+    for k in range(1, chunks):
+        load_right(k, 0).start()
+        if k == 1:
+            load_amps.start()
 
     barrier = pltpu.get_barrier_semaphore()
 
@@ -59,42 +57,36 @@
             barrier, inc=1, device_id={"row": lax.rem(me + k, n)}, device_id_type=MESH
         )
 
-    turn = 2
-    for p in range(LEFT_PIECES):
-        load_left(p).wait()
-
-        @pl.loop(0, left_lanes // (LEFT_PIECES * turn))
-        def _(t):
-            for e in range(turn):
-                at = p * (left_lanes // LEFT_PIECES) + t * turn + e
-                lanes = pl.ds(pl.multiple_of(at * LANES, LANES), LANES)
-                staged = left_f32[e]
-                staged[...] = (
-                    left_in[:, :, lanes].astype(jnp.float32).reshape(count_a * c_block, LANES)
-                )
-                for c in range(c_block):
-                    left_rows[pl.ds(c * count_a, count_a), lanes] = staged[
-                        pl.ds(c, count_a, stride=c_block), :
-                    ].astype(jnp.bfloat16)
-
-    def split_right(k, kt):
-        staged, columns = right_f32[k % 2], right_cols[k % 2]
+    def split_left(kt):
+        load_left(kt).wait()
+        for e in range(TILE // LANES):
+            lanes = pl.ds(kt * TILE + e * LANES, LANES)
+            staged = left_f32[e]
+            staged[...] = (
+                left_in[:, :, lanes].astype(jnp.float32).reshape(count_a * c_block, LANES)
+            )
+            for c in range(c_block):
+                left_rows[pl.ds(c * count_a, count_a), lanes] = staged[
+                    pl.ds(c, count_a, stride=c_block), :
+                ].astype(jnp.bfloat16)
+
+    def stage_right(i):
+        k, kt = divmod(i, q_tiles)
+        if k == 0 or kt == 0:
+            load_right(k, kt).wait()
         flat = right_in.at[k].reshape(naux * count_b, LANES)
-        step = 64
-        for s in range(kt * TILE // step, (kt + 1) * TILE // step):
-            rows = pl.ds(s * step * count_b, step * count_b)
-            staged[rows, :] = flat[rows, :].astype(jnp.float32)
-            for b in range(count_b):
-                columns[pl.ds(s * step, step), pl.ds(b * LANES, LANES)] = staged[
-                    pl.ds(s * step * count_b + b, step, stride=count_b), :
-                ].astype(jnp.bfloat16)
-
-    def split_amps(k, kt):
+        right_f32[i % len(right_f32)][...] = flat[
+            pl.ds(kt * TILE * count_b, TILE * count_b), :
+        ].astype(jnp.float32)
+
+    def split_amps(k, part, parts):
         lanes = pl.ds(k * LANES, LANES)
         staged = amps_f32[k % 2]
-        if kt == 0:
+        if part == 0:
+            if k == 0:
+                load_amps.wait()
             staged[...] = amps_in[:, :, lanes].astype(jnp.float32).reshape(pairs * c_block, LANES)
-        for c in range(kt * c_block // q_tiles, (kt + 1) * c_block // q_tiles):
+        for c in range(part * c_block // parts, (part + 1) * c_block // parts):
             picked = staged[pl.ds(c, pairs, stride=c_block), :].astype(jnp.bfloat16)
             for f in range(fold):
                 amps_rows[k % 2][
@@ -120,9 +112,12 @@
 
     def integrate(acc, k, kt):
         def push(m, staging):
-            pltpu.matmul_push_rhs(
-                right_cols[k % 2][pl.ds(kt * TILE, TILE), pl.ds(m * TILE, TILE)], staging, m
-            )
+            rows = right_f32[(k * q_tiles + kt) % len(right_f32)]
+            tile = [
+                rows[pl.ds(m * (count_b // 2) + e, TILE, stride=count_b), :].astype(jnp.bfloat16)
+                for e in range(count_b // 2)
+            ]
+            pltpu.matmul_push_rhs(jnp.concatenate(tile, axis=1), staging, m)
 
         def multiply(m, staging):
             for h in range(m_halves):
@@ -156,34 +151,33 @@
 
         return push, multiply, lambda: None
 
-    def arrived(k):
-        if k + 1 < chunks:
-            load_right(k + 1).wait()
-        if k == 0:
-            load_amps.wait()
-
     def on_units(acc, acc_out):
         tiles = []
+        last = chunks * q_tiles
+        half = q_tiles // 2
         for k in range(chunks):
             for kt in range(q_tiles):
+                i = k * q_tiles + kt
                 beside = []
-                if k + 1 < chunks:
-                    beside.append(functools.partial(split_right, k + 1, kt))
-                beside.append(functools.partial(split_amps, k, kt))
-                before = functools.partial(arrived, k) if kt == 0 else None
-                tiles.append((integrate(acc, k, kt), before, beside))
-                if k > 0 and kt in (1, 2):
-                    tiles.append((contract(acc_out, k - 1, kt - 1), None, []))
-        tiles += [(contract(acc_out, chunks - 1, p), None, []) for p in range(2)]
-
-        load_right(0).wait()
-        for kt in range(q_tiles):
-            split_right(0, kt)
+                if i + 1 < q_tiles:
+                    beside.append(functools.partial(split_left, i + 1))
+                if i + 2 < last:
+                    beside.append(functools.partial(stage_right, i + 2))
+                if k > 0 and kt < half:
+                    beside.append(functools.partial(split_amps, k - 1, kt, half))
+                if k == chunks - 1 and kt >= half:
+                    beside.append(functools.partial(split_amps, k, kt - half, q_tiles - half))
+                tiles.append((integrate(acc, k, kt), beside))
+                if k > 0 and kt in (half, half + 1):
+                    tiles.append((contract(acc_out, k - 1, kt - half), []))
+        tiles += [(contract(acc_out, chunks - 1, p), []) for p in range(2)]
+
+        stage_right(0)
+        split_left(0)
+        stage_right(1)
         for m in range(2):
             tiles[0][0][0](m, 0)
-        for i, ((_, multiply, finish), before, beside) in enumerate(tiles):
-            if before is not None:
-                before()
+        for i, ((_, multiply, finish), beside) in enumerate(tiles):
             if i + 1 < len(tiles):
                 for m in range(2):
                     tiles[i + 1][0][0](m, (i + 1) % 2)
@@ -261,13 +255,14 @@
             pltpu.VMEM((c_block * count_a, naux), bf16),
             [pltpu.VMEM((pairs * c_block, LANES), f32)] * 2,
             [pltpu.VMEM((c_block // 2 * fold * pairs, TILE), bf16)] * 2,
-            [pltpu.VMEM((naux * count_b, LANES), f32)] * 2,
-            [pltpu.VMEM((naux, count_b * LANES), bf16)] * 2,
+            [pltpu.VMEM((TILE * count_b, LANES), f32)] * 4,
             [pltpu.VMEM((c_block * count_a, count_b * LANES), bf16)] * 2,
             pltpu.VMEM((count_b * count_a, fold * pairs), f32),
             pltpu.VMEM((count_a,) + piece, f32),
             pltpu.VMEM(((n - 1) * own_a,) + piece, f32),
-            pltpu.SemaphoreType.DMA((1 + width // LANES + LEFT_PIECES,)),
+            pltpu.SemaphoreType.DMA((naux // TILE,)),
+            pltpu.SemaphoreType.DMA((naux // TILE + width // LANES - 1,)),
+            pltpu.SemaphoreType.DMA,
             pltpu.SemaphoreType.DMA,
             pltpu.SemaphoreType.DMA,
         ],

time: 18.7 us -> 17.6 us (0.941)
  Pallas kernels: 18 us -> 16.9 us
    pallas_call x1, Pallas kernels: 18 us -> 16.9 us  [per_device(): pl.pallas_call(functools.partial(ladder_kernel, n, fold), out_shape=jax.S...]
where the time goes in v5:
time: 17.6 us; the launch traced here: 17.5 us
  Pallas kernels  16.9 us (96%)
  local copies, waits for them, and re-layouts  0.58 us (3%)
    pallas_call x1, Pallas kernels, per_device(): pl.pallas_call(functools.partial(ladder_kernel, n, fold), out_shape=jax.S...  16.9 us
    unnamed x1, local copies, waits for them, and re-layouts  0.58 us

profile of v5, /device:TPU:0, one launch (start us, length us, event | category | flops | bytes accessed | tf_op | source)
XLA Modules:
  0.0 17.5 jit_solution(9434902138370632092)
XLA Ops:
  0.0 16.9 %ladder.1 = f32[1,4,64]{2,1,0:T(4,128)S(1)} custom-call(bf16[32,16,1536]{2,1,0:T(8,128)(2,1)} %bitcast.3, bf16[1536,4,512]{2,1,0:T(4,128)(2,1)} %right_hbm, bf16[64,16,512]{2,1,0:T(8,128)(2,1)} %amps_hbm.1), custom_call_target="tpu_custom_call" | custom-call | tf_op jit(solution)/shard_map/ladder/pallas_call | solution.py:245
  16.9 0.6 %copy.5 = f32[64,1,4]{0,2,1:T(4,128)} copy(f32[64,1,4]{0,2,1:T(4,128)S(1)} %bitcast.2) | data formatting | bytes 2048

commit v6 on v1

v6 whole, which is shorter than its diff:
```python
import functools

import jax
import jax.numpy as jnp
from jax import lax
from jax.experimental import pallas as pl
from jax.experimental.pallas import tpu as pltpu
from jax.sharding import PartitionSpec as P

MESH = pl.DeviceIdType.MESH
LANES = 128
TILE = 256


def ladder_kernel(
    n, fold, left_hbm, right_hbm, amps_hbm, out_ref,
    left_in, amps_in, right_in, picks, left_rows, amps_rows, right_cols,
    integrals, total_buf, send_buf, recv_buf, left_sem, right_sem, amps_sem, send_sem, recv_sem,
):
    count_a, c_block, naux = left_hbm.shape
    _, count_b, width = right_hbm.shape
    pairs = amps_hbm.shape[0]
    chunks = width // LANES
    own_a = count_a // n
    me = lax.axis_index("row")

    q_tiles = naux // TILE

    def load_left(kt):
        lanes = pl.ds(kt * TILE, TILE)
        return pltpu.make_async_copy(
            left_hbm.at[:, :, lanes], left_in.at[:, :, lanes], left_sem.at[kt]
        )

    def load_right(k, kt):
        early = k < 2
        rows = pl.ds(kt * TILE, TILE) if early else slice(None)
        return pltpu.make_async_copy(
            right_hbm.at[rows, :, pl.ds(k * LANES, LANES)], right_in.at[k, rows],
            right_sem.at[k * q_tiles + kt if early else 2 * q_tiles + k - 2],
        )

    load_amps = pltpu.make_async_copy(amps_hbm, amps_in, amps_sem)
    for kt in range(q_tiles):
        load_left(kt).start()
        for k in range(2):
            load_right(k, kt).start()
    for k in range(2, chunks):
        load_right(k, 0).start()
    load_amps.start()

    barrier = pltpu.get_barrier_semaphore()

    @pl.loop(1, n)
    def _(k):
        pl.semaphore_signal(
            barrier, inc=1, device_id={"row": lax.rem(me + k, n)}, device_id_type=MESH
        )

    i = lax.broadcasted_iota(jnp.int32, (TILE, TILE), 0)
    j = lax.broadcasted_iota(jnp.int32, (TILE, TILE), 1)
    q_rows = TILE // count_b
    outer = TILE // c_block
    picks[0] = (j == (i % q_rows) * count_b + i // q_rows).astype(jnp.bfloat16)
    picks[1] = (j == (i % outer) * c_block + i // outer).astype(jnp.bfloat16)

    def on_units(acc, moved):
        def move(which, slot, source, store, wait):
            def push(staging):
                wait()
                for m in range(2):
                    pltpu.matmul_push_rhs(source(m), staging, m)

            def multiply(staging):
                for m in range(2):
                    pltpu.matmul_acc_lhs(moved[m][slot], picks[which], load_staged_rhs=staging)

            def finish():
                for m in range(2):
                    store(m, pltpu.matmul_pop(moved[m][slot]).astype(jnp.bfloat16))

            return push, multiply, finish, ("moved", slot)

        def move_left(kt, slot):
            lanes = pl.ds(kt * TILE, TILE)

            def source(m):
                return left_in[pl.ds(m * outer, outer), :, lanes].reshape(TILE, TILE)

            def store(m, value):
                left_rows[pl.ds(m * TILE, TILE), lanes] = value

            return move(1, slot, source, store, lambda: load_left(kt).wait())

        def move_right(kk, kt, part, slot):
            def at(m):
                return kt * count_b + part * 2 + m

            def source(m):
                return jnp.concatenate(
                    [
                        right_in.at[2 * kk + e].reshape(naux * count_b, LANES)[
                            pl.ds(at(m) * TILE, TILE), :
                        ]
                        for e in range(2)
                    ],
                    axis=1,
                )

            def store(m, value):
                for b in range(count_b):
                    right_cols[kk][pl.ds(at(m) * q_rows, q_rows), pl.ds(b * TILE, TILE)] = value[
                        b * q_rows : (b + 1) * q_rows
                    ]

            def wait():
                if part == 0 and (kk == 0 or kt == 0):
                    for e in range(2):
                        load_right(2 * kk + e, kt).wait()

            return move(0, slot, source, store, wait)

        def move_amps(kk, part, slot):
            lanes = pl.ds(kk * TILE, TILE)

            def source(m):
                block = part * 2 + m
                return amps_in[pl.ds(block * outer, outer), :, lanes].reshape(TILE, TILE)

            def store(m, value):
                block = part * 2 + m
                for c in range(c_block):
                    amps_rows[kk][pl.ds(c * pairs + block * outer, outer), :] = value[
                        c * outer : (c + 1) * outer
                    ]

            def wait():
                if kk == 0 and part == 0:
                    load_amps.wait()

            return move(1, slot, source, store, wait)

        rows_of = count_a * c_block // len(acc[0])

        def integrate(kk, bb, kt):
            def push(staging):
                for m in range(2):
                    pltpu.matmul_push_rhs(
                        right_cols[kk][pl.ds(kt * TILE, TILE), pl.ds((2 * bb + m) * TILE, TILE)],
                        staging, m,
                    )

            def multiply(staging):
                for h in range(len(acc[0])):
                    for m in range(2):
                        pltpu.matmul_acc_lhs(
                            acc[m][h],
                            left_rows[pl.ds(h * rows_of, rows_of), pl.ds(kt * TILE, TILE)],
                            load_staged_rhs=staging if h == 0 else None,
                        )

            def finish():
                if kt == q_tiles - 1:
                    for h in range(len(acc[0])):
                        for m in range(2):
                            integrals[kk][
                                pl.ds(h * rows_of, rows_of), pl.ds((2 * bb + m) * TILE, TILE)
                            ] = pltpu.matmul_pop(acc[m][h]).astype(jnp.bfloat16)

            return push, multiply, finish, "acc" if kt == q_tiles - 1 else None

        def contract(kk, part):
            def group(m):
                return part * 2 + m

            def push(staging):
                for m in range(2):
                    pltpu.matmul_push_rhs(
                        amps_rows[kk][pl.ds(group(m) * TILE, TILE), :], staging, m, transpose=True
                    )

            def multiply(staging):
                for e in range(len(acc[0])):
                    for m in range(2):
                        c = group(m) * len(acc[0]) + e
                        block = [
                            integrals[kk][
                                pl.ds(h * TILE + c * outer, outer), pl.ds(b * TILE, TILE)
                            ]
                            for b in range(count_b)
                            for h in range(count_a // outer)
                        ]
                        pltpu.matmul_acc_lhs(
                            acc[m][e], jnp.concatenate(block, axis=0),
                            load_staged_rhs=staging if e == 0 else None,
                        )

            return push, multiply, lambda: None, None

        made = [0]

        def slot():
            made[0] += 1
            return made[0] % 2

        def moves(kt):
            return [move_left(kt, slot())] + [move_right(0, kt, p, slot()) for p in range(2)]

        tiles = moves(0) + moves(1)
        rest = [(kt, p) for kt in range(q_tiles) for p in range(2)]
        for kt in range(q_tiles):
            tiles.append(integrate(0, 0, kt))
            if kt + 2 < q_tiles:
                tiles += moves(kt + 2)
            else:
                tiles += [move_right(1, *rest.pop(0), slot()) for _ in range(2)]
        for kt in range(q_tiles):
            tiles.append(integrate(0, 1, kt))
            tiles += [move_right(1, *rest.pop(0), slot()) for _ in range(min(2, len(rest)))]
        later = [(kk, p) for kk in range(2) for p in range(2)]
        tiles.append(move_amps(*later.pop(0), slot()))
        for bb in range(2):
            for kt in range(q_tiles):
                tiles.append(integrate(1, bb, kt))
                if kt >= 3 and later:
                    tiles.append(move_amps(*later.pop(0), slot()))
        for kk in range(2):
            tiles += [contract(kk, p) for p in range(2)]

        pending = None
        tiles[0][0](0)
        for n_tile, (_, multiply, finish, key) in enumerate(tiles):
            if n_tile + 1 < len(tiles):
                tiles[n_tile + 1][0]((n_tile + 1) % 2)
            if pending is not None and pending[1] == "acc" and not isinstance(key, tuple):
                pending[0]()
                pending = None
            multiply(n_tile % 2)
            if pending is not None:
                pending[0]()
            pending = (finish, key)

        low, high = 0.0, 0.0
        for m in range(2):
            for e in range(len(acc[0])):
                lanes = e * pairs // LANES * LANES
                value = pltpu.matmul_pop(acc[m][e])[:, lanes : lanes + LANES]
                low, high = (low + value, high) if e % 2 == 0 else (low, high + value)
        lane = lax.broadcasted_iota(jnp.int32, low.shape, 1)
        both = jnp.where(lane < pairs, low, high)
        total_buf[...] = both + pltpu.roll(both, pairs, 1)

    pl.run_scoped(
        on_units,
        [
            [pltpu.ACC(m)((count_a * count_b, TILE), jnp.float32)] * (TILE // pairs)
            for m in range(2)
        ],
        [[pltpu.ACC(m)((TILE, TILE), jnp.float32)] * 2 for m in range(2)],
    )
    total = total_buf[...]

    lane = lax.broadcasted_iota(jnp.int32, (count_a, fold * pairs), 1)
    for g in range(count_b // fold):
        row = total[g * fold * count_a : (g * fold + 1) * count_a]
        for f in range(1, fold):
            b = g * fold + f
            row = jnp.where(lane >= f * pairs, total[b * count_a : (b + 1) * count_a], row)
        send_buf[:, g, :] = row

    pl.semaphore_wait(barrier, n - 1)

    @pl.loop(1, n)
    def _(k):
        to = lax.rem(me + k, n)
        pltpu.make_async_remote_copy(
            src_ref=send_buf.at[pl.ds(to * own_a, own_a)],
            dst_ref=recv_buf.at[pl.ds((k - 1) * own_a, own_a)],
            send_sem=send_sem,
            recv_sem=recv_sem,
            device_id={"row": to},
            device_id_type=MESH,
        ).start()

    every = recv_buf.at[pl.ds(0, (n - 1) * own_a)]
    pltpu.make_async_copy(every, every, recv_sem).wait()
    mine = send_buf[pl.ds(me * own_a, own_a)]
    got = recv_buf[...].reshape((n - 1, own_a) + recv_buf.shape[1:])
    result = mine + jnp.sum(got, axis=0)
    for b in range(count_b):
        out_ref[:, b, :] = result[:, b // fold, (b % fold) * pairs : (b % fold + 1) * pairs]
    pltpu.make_async_copy(every, every, send_sem).wait()


def per_device(n, left_factors, right_factors, amplitudes):
    left = lax.all_gather(left_factors, "col", axis=0, tiled=True)
    right = lax.all_gather(right_factors, "col", axis=0, tiled=True)
    naux, count_a, c_block = left.shape
    _, count_b, width = right.shape
    pairs = amplitudes.shape[0]
    fold = 2 if 2 * pairs == LANES and count_b % 2 == 0 else 1
    own_a = count_a // n
    anywhere = pl.BlockSpec(memory_space=pl.ANY)
    bf16, f32 = jnp.bfloat16, jnp.float32
    piece = (count_b // fold, fold * pairs)
    out = pl.pallas_call(
        functools.partial(ladder_kernel, n, fold),
        out_shape=jax.ShapeDtypeStruct((own_a, count_b, pairs), f32),
        in_specs=[anywhere] * 3,
        out_specs=pl.BlockSpec(memory_space=pltpu.VMEM),
        scratch_shapes=[
            pltpu.VMEM((count_a, c_block, naux), bf16),
            pltpu.VMEM((pairs, c_block, width), bf16),
            pltpu.VMEM((width // LANES, naux, count_b, LANES), bf16),
            pltpu.VMEM((2, TILE, TILE), bf16),
            pltpu.VMEM((c_block * count_a, naux), bf16),
            [pltpu.VMEM((c_block * pairs, TILE), bf16)] * (width // TILE),
            [pltpu.VMEM((naux, count_b * TILE), bf16)] * (width // TILE),
            [pltpu.VMEM((c_block * count_a, count_b * TILE), bf16)] * (width // TILE),
            pltpu.VMEM((count_b * count_a, fold * pairs), f32),
            pltpu.VMEM((count_a,) + piece, f32),
            pltpu.VMEM(((n - 1) * own_a,) + piece, f32),
            pltpu.SemaphoreType.DMA((naux // TILE,)),
            pltpu.SemaphoreType.DMA((2 * (naux // TILE) + width // LANES - 2,)),
            pltpu.SemaphoreType.DMA,
            pltpu.SemaphoreType.DMA,
            pltpu.SemaphoreType.DMA,
        ],
        compiler_params=pltpu.CompilerParams(
            collective_id=0, has_side_effects=True, vmem_limit_bytes=53 * 1024 * 1024
        ),
        name="ladder",
    )(jnp.transpose(left, (1, 2, 0)), right, amplitudes)
    return jnp.transpose(out, (2, 0, 1))


def solution(mesh):
    placed = (P("col", None, "row"), P("col", None, None), P("col", "row", None))
    return jax.shard_map(
        functools.partial(per_device, mesh.shape["row"]),
        mesh=mesh, in_specs=placed, out_specs=P("col", "row", None), check_vma=False,
    )
```

time: 21.6 us -> 18.4 us (0.85)
  local copies, waits for them, and re-layouts: 3.21 us -> 0.58 us
  Pallas kernels: 18.2 us -> 17.7 us
    unnamed x5 -> x1, local copies, waits for them, and re-layouts: 3.21 us -> 0.58 us
    pallas_call x1, Pallas kernels: 18.2 us -> 17.7 us  [per_device(): pl.pallas_call(functools.partial(ladder_kernel, n, fold), out_shape=jax.S...]
where the time goes in v6:
time: 18.4 us; the launch traced here: 18.3 us
  Pallas kernels  17.7 us (96%)
  local copies, waits for them, and re-layouts  0.58 us (3%)
    pallas_call x1, Pallas kernels, per_device(): pl.pallas_call(functools.partial(ladder_kernel, n, fold), out_shape=jax.S...  17.7 us
    unnamed x1, local copies, waits for them, and re-layouts  0.58 us

profile of v6, /device:TPU:0, one launch (start us, length us, event | category | flops | bytes accessed | tf_op | source)
XLA Modules:
  0.0 18.3 jit_solution(10408361188072948387)
XLA Ops:
  0.0 17.7 %ladder.1 = f32[1,4,64]{2,1,0:T(4,128)S(1)} custom-call(bf16[32,16,1536]{2,1,0:T(8,128)(2,1)} %bitcast.3, bf16[1536,4,512]{2,1,0:T(4,128)(2,1)} %right_hbm, bf16[64,16,512]{2,1,0:T(8,128)(2,1)} %amps_hbm.1), custom_call_target="tpu_custom_call" | custom-call | tf_op jit(solution)/shard_map/ladder/pallas_call | solution.py:306
  17.7 0.6 %copy.5 = f32[64,1,4]{0,2,1:T(4,128)} copy(f32[64,1,4]{0,2,1:T(4,128)S(1)} %bitcast.2) | data formatting | bytes 2048

commit v7 on v5

--- a/solution.py
+++ b/solution.py
@@ -14,7 +14,7 @@
 
 def ladder_kernel(
     n, fold, left_hbm, right_hbm, amps_hbm, out_ref,
-    left_in, amps_in, right_in, left_f32, left_rows, amps_f32, amps_rows, right_f32,
+    left_in, amps_in, right_in, pick, left_rows, amps_f32, amps_rows, right_f32,
     integrals, total_buf, send_buf, recv_buf, left_sem, right_sem, amps_sem, send_sem, recv_sem,
 ):
     count_a, c_block, naux = left_hbm.shape
@@ -34,10 +34,10 @@
         )
 
     def load_right(k, kt):
-        rows = pl.ds(kt * TILE, TILE) if k == 0 else slice(None)
+        rows = pl.ds(kt * TILE, TILE)
         return pltpu.make_async_copy(
             right_hbm.at[rows, :, pl.ds(k * LANES, LANES)], right_in.at[k, rows],
-            right_sem.at[kt if k == 0 else q_tiles - 1 + k],
+            right_sem.at[k * q_tiles + kt],
         )
 
     load_amps = pltpu.make_async_copy(amps_hbm, amps_in, amps_sem)
@@ -45,7 +45,8 @@
         load_left(kt).start()
         load_right(0, kt).start()
     for k in range(1, chunks):
-        load_right(k, 0).start()
+        for kt in range(q_tiles):
+            load_right(k, kt).start()
         if k == 1:
             load_amps.start()
 
@@ -57,23 +58,35 @@
             barrier, inc=1, device_id={"row": lax.rem(me + k, n)}, device_id_type=MESH
         )
 
-    def split_left(kt):
-        load_left(kt).wait()
-        for e in range(TILE // LANES):
-            lanes = pl.ds(kt * TILE + e * LANES, LANES)
-            staged = left_f32[e]
-            staged[...] = (
-                left_in[:, :, lanes].astype(jnp.float32).reshape(count_a * c_block, LANES)
+    outer = TILE // c_block
+    i = lax.broadcasted_iota(jnp.int32, (TILE, TILE), 0)
+    j = lax.broadcasted_iota(jnp.int32, (TILE, TILE), 1)
+    pick[...] = (j == (i % outer) * c_block + i // outer).astype(jnp.bfloat16)
+
+    def move_left(moved, kt):
+        lanes = pl.ds(kt * TILE, TILE)
+
+        def push(m, staging):
+            if m == 0:
+                load_left(kt).wait()
+            pltpu.matmul_push_rhs(
+                left_in[pl.ds(m * outer, outer), :, lanes].reshape(TILE, TILE), staging, m
             )
-            for c in range(c_block):
-                left_rows[pl.ds(c * count_a, count_a), lanes] = staged[
-                    pl.ds(c, count_a, stride=c_block), :
-                ].astype(jnp.bfloat16)
+
+        def multiply(m, staging):
+            pltpu.matmul_acc_lhs(moved[m], pick[...], load_staged_rhs=staging)
+
+        def finish():
+            for m in range(2):
+                left_rows[pl.ds(m * TILE, TILE), lanes] = pltpu.matmul_pop(moved[m]).astype(
+                    jnp.bfloat16
+                )
+
+        return push, multiply, finish
 
     def stage_right(i):
         k, kt = divmod(i, q_tiles)
-        if k == 0 or kt == 0:
-            load_right(k, kt).wait()
+        load_right(k, kt).wait()
         flat = right_in.at[k].reshape(naux * count_b, LANES)
         right_f32[i % len(right_f32)][...] = flat[
             pl.ds(kt * TILE * count_b, TILE * count_b), :
@@ -99,13 +112,14 @@
                 jnp.concatenate(
                     [
                         integrals[k % 2][
-                            pl.ds((g * 2 + e) * count_a, count_a), pl.ds(b * LANES, LANES)
+                            pl.ds(h * TILE + (g * 2 + e) * outer, outer), pl.ds(b * LANES, LANES)
                         ]
                         for e in range(2)
                     ],
                     axis=1,
                 )
                 for b in range(count_b)
+                for h in range(m_halves)
             ],
             axis=0,
         )
@@ -151,16 +165,14 @@
 
         return push, multiply, lambda: None
 
-    def on_units(acc, acc_out):
-        tiles = []
+    def on_units(acc, acc_out, moved):
+        tiles = [(move_left(moved, kt), None) for kt in range(2)]
         last = chunks * q_tiles
         half = q_tiles // 2
         for k in range(chunks):
             for kt in range(q_tiles):
                 i = k * q_tiles + kt
                 beside = []
-                if i + 1 < q_tiles:
-                    beside.append(functools.partial(split_left, i + 1))
                 if i + 2 < last:
                     beside.append(functools.partial(stage_right, i + 2))
                 if k > 0 and kt < half:
@@ -168,24 +180,33 @@
                 if k == chunks - 1 and kt >= half:
                     beside.append(functools.partial(split_amps, k, kt - half, q_tiles - half))
                 tiles.append((integrate(acc, k, kt), beside))
+                if i + 2 < q_tiles:
+                    tiles.append((move_left(moved, i + 2), None))
                 if k > 0 and kt in (half, half + 1):
                     tiles.append((contract(acc_out, k - 1, kt - half), []))
         tiles += [(contract(acc_out, chunks - 1, p), []) for p in range(2)]
 
         stage_right(0)
-        split_left(0)
         stage_right(1)
         for m in range(2):
             tiles[0][0][0](m, 0)
+        late = None
         for i, ((_, multiply, finish), beside) in enumerate(tiles):
             if i + 1 < len(tiles):
                 for m in range(2):
                     tiles[i + 1][0][0](m, (i + 1) % 2)
+            if late is not None and beside is None:
+                late()
+                late = None
             for m in range(2):
                 multiply(m, i % 2)
-            for run in beside:
+            for run in beside or []:
                 run()
-            finish()
+            if late is not None:
+                late()
+            late = finish if beside is None else None
+            if late is None:
+                finish()
         total = 0.0
         for m in range(2):
             for e in range(2):
@@ -196,6 +217,7 @@
         on_units,
         [[pltpu.ACC(m)((TILE, TILE), jnp.float32)] * m_halves for m in range(2)],
         [[pltpu.ACC(m)((count_a * count_b, TILE), jnp.float32)] * 2 for m in range(2)],
+        [pltpu.ACC(m)((TILE, TILE), jnp.float32) for m in range(2)],
     )
     total = total_buf[...]
 
@@ -251,7 +273,7 @@
             pltpu.VMEM((count_a, c_block, naux), bf16),
             pltpu.VMEM((pairs, c_block, width), bf16),
             pltpu.VMEM((width // LANES, naux, count_b, LANES), bf16),
-            [pltpu.VMEM((count_a * c_block, LANES), f32)] * 2,
+            pltpu.VMEM((TILE, TILE), bf16),
             pltpu.VMEM((c_block * count_a, naux), bf16),
             [pltpu.VMEM((pairs * c_block, LANES), f32)] * 2,
             [pltpu.VMEM((c_block // 2 * fold * pairs, TILE), bf16)] * 2,
@@ -261,7 +283,7 @@
             pltpu.VMEM((count_a,) + piece, f32),
             pltpu.VMEM(((n - 1) * own_a,) + piece, f32),
             pltpu.SemaphoreType.DMA((naux // TILE,)),
-            pltpu.SemaphoreType.DMA((naux // TILE + width // LANES - 1,)),
+            pltpu.SemaphoreType.DMA((naux // TILE * (width // LANES),)),
             pltpu.SemaphoreType.DMA,
             pltpu.SemaphoreType.DMA,
             pltpu.SemaphoreType.DMA,

time: 17.6 us -> 18.9 us (1.074)
  Pallas kernels: 16.9 us -> 18.2 us
    pallas_call x1, Pallas kernels: 16.9 us -> 18.2 us  [per_device(): pl.pallas_call(functools.partial(ladder_kernel, n, fold), out_shape=jax.S...]
where the time goes in v7:
time: 18.9 us; the launch traced here: 18.7 us
  Pallas kernels  18.2 us (96%)
  local copies, waits for them, and re-layouts  0.58 us (3%)
    pallas_call x1, Pallas kernels, per_device(): pl.pallas_call(functools.partial(ladder_kernel, n, fold), out_shape=jax.S...  18.2 us
    unnamed x1, local copies, waits for them, and re-layouts  0.58 us

profile of v7, /device:TPU:0, one launch (start us, length us, event | category | flops | bytes accessed | tf_op | source)
XLA Modules:
  0.0 18.7 jit_solution(5087874307976597130)
XLA Ops:
  0.0 18.2 %ladder.1 = f32[1,4,64]{2,1,0:T(4,128)S(1)} custom-call(bf16[32,16,1536]{2,1,0:T(8,128)(2,1)} %bitcast.3, bf16[1536,4,512]{2,1,0:T(4,128)(2,1)} %right_hbm, bf16[64,16,512]{2,1,0:T(8,128)(2,1)} %amps_hbm.1), custom_call_target="tpu_custom_call" | custom-call | tf_op jit(solution)/shard_map/ladder/pallas_call | solution.py:267
  18.2 0.6 %copy.5 = f32[64,1,4]{0,2,1:T(4,128)} copy(f32[64,1,4]{0,2,1:T(4,128)S(1)} %bitcast.2) | data formatting | bytes 2048

commit v8 on v5

--- a/solution.py
+++ b/solution.py
@@ -27,23 +27,25 @@
     q_tiles = naux // TILE
     m_halves = count_a * c_block // TILE
 
-    def load_left(kt):
-        lanes = pl.ds(kt * TILE, TILE)
+    group = 2 if q_tiles % 2 == 0 else 1
+
+    def load_left(p):
+        lanes = pl.ds(p * group * TILE, group * TILE)
         return pltpu.make_async_copy(
-            left_hbm.at[:, :, lanes], left_in.at[:, :, lanes], left_sem.at[kt]
-        )
-
-    def load_right(k, kt):
-        rows = pl.ds(kt * TILE, TILE) if k == 0 else slice(None)
+            left_hbm.at[:, :, lanes], left_in.at[:, :, lanes], left_sem.at[p]
+        )
+
+    def load_right(k, p):
+        rows = pl.ds(p * group * TILE, group * TILE) if k == 0 else slice(None)
         return pltpu.make_async_copy(
             right_hbm.at[rows, :, pl.ds(k * LANES, LANES)], right_in.at[k, rows],
-            right_sem.at[kt if k == 0 else q_tiles - 1 + k],
+            right_sem.at[p if k == 0 else q_tiles - 1 + k],
         )
 
     load_amps = pltpu.make_async_copy(amps_hbm, amps_in, amps_sem)
-    for kt in range(q_tiles):
-        load_left(kt).start()
-        load_right(0, kt).start()
+    for p in range(q_tiles // group):
+        load_left(p).start()
+        load_right(0, p).start()
     for k in range(1, chunks):
         load_right(k, 0).start()
         if k == 1:
@@ -58,7 +60,6 @@
         )
 
     def split_left(kt):
-        load_left(kt).wait()
         for e in range(TILE // LANES):
             lanes = pl.ds(kt * TILE + e * LANES, LANES)
             staged = left_f32[e]
@@ -72,8 +73,11 @@
 
     def stage_right(i):
         k, kt = divmod(i, q_tiles)
-        if k == 0 or kt == 0:
-            load_right(k, kt).wait()
+        if k == 0 and kt % group == 0:
+            load_left(kt // group).wait()
+            load_right(k, kt // group).wait()
+        elif k > 0 and kt == 0:
+            load_right(k, 0).wait()
         flat = right_in.at[k].reshape(naux * count_b, LANES)
         right_f32[i % len(right_f32)][...] = flat[
             pl.ds(kt * TILE * count_b, TILE * count_b), :

time: 17.6 us -> 17.6 us (level)
  no operation moved by 1% of the time
where the time goes in v8:
time: 17.6 us; the launch traced here: 17.4 us
  Pallas kernels  16.8 us (95%)
  local copies, waits for them, and re-layouts  0.58 us (3%)
    pallas_call x1, Pallas kernels, per_device(): pl.pallas_call(functools.partial(ladder_kernel, n, fold), out_shape=jax.S...  16.8 us
    unnamed x1, local copies, waits for them, and re-layouts  0.58 us

profile of v8, /device:TPU:0, one launch (start us, length us, event | category | flops | bytes accessed | tf_op | source)
XLA Modules:
  0.0 17.4 jit_solution(13953367583396416842)
XLA Ops:
  0.0 16.8 %ladder.1 = f32[1,4,64]{2,1,0:T(4,128)S(1)} custom-call(bf16[32,16,1536]{2,1,0:T(8,128)(2,1)} %bitcast.3, bf16[1536,4,512]{2,1,0:T(4,128)(2,1)} %right_hbm, bf16[64,16,512]{2,1,0:T(8,128)(2,1)} %amps_hbm.1), custom_call_target="tpu_custom_call" | custom-call | tf_op jit(solution)/shard_map/ladder/pallas_call | solution.py:249
  16.9 0.6 %copy.5 = f32[64,1,4]{0,2,1:T(4,128)} copy(f32[64,1,4]{0,2,1:T(4,128)S(1)} %bitcast.2) | data formatting | bytes 2048
